TPU v7x, 32 devices: a whole 2x2x4 slice. The times are simulated.
32 devices in a mesh: frame: 16 (over z, y, core), head: 2 (over x).
Axes of the slice: x: 2, y: 2, z: 4, core: 2. Of those that a mesh axis runs over, the one named last changes fastest.
Arguments:
- queries: bfloat16 [16384, 3072], P(('frame', 'head')), may hold values from -64 to 64, as said below
- key_rows: bfloat16 [16384, 3072], P(('frame', 'head')), may hold values from -64 to 64, as said below
- value_rows: bfloat16 [16384, 3072], P(('frame', 'head')), may hold values from -24 to 24
- block_mask: int32 [128, 128], replicated, may hold values from 0 to 1, as said below
Outputs:
- attended: bfloat16 [16384, 3072], P(('frame', 'head'))
Inputs may be any that keep to these rules, and one draw needn't show every extreme that they name: block_mask holds 0 or 1; every query block attends to all key blocks of its own frame; for two frames two or more apart, the query blocks of one attend to exactly one key block of the other (the same one for all of them), and some query blocks may attend to none of it. queries are finite reals. `key_rows`: keys are finite reals.
All inputs are finite; a program needn't handle non-finite values.
Results may differ from a plain program's by a relative error of at most 0.0037.
Values may be sent and summed in bfloat16 or wider, within the bound.
A program may use at most 192 MiB of HBM per device.

v0:
```python
import math

import jax
import jax.numpy as jnp
from jax import lax
from jax.sharding import PartitionSpec as P

HDIM = 128
BLOCK = 128
BF = 8


def padded(value, sides, width):
    for axis, dim in sides:
        peers, length = (lax.axis_size(axis), value.shape[dim])
        up = [(i, (i + 1) % peers) for i in range(peers - 1)]
        down = [(j, i) for i, j in up]
        last = lax.slice_in_dim(value, length - width, length, axis=dim)
        first = lax.slice_in_dim(value, 0, width, axis=dim)
        before = lax.ppermute(last, axis, up)
        after = lax.ppermute(first, axis, down)
        value = jnp.concatenate([before, value, after], axis=dim)
    return value


def masked_scores(query_part, key_part, block_rows, score_scale):
    scores = (
        jnp.einsum("thd,uhd->htu", query_part, key_part, preferred_element_type=jnp.float32)
        * score_scale
    )
    heads, rows, cols = scores.shape
    shaped = scores.reshape(heads, rows // BLOCK, BLOCK, cols // BLOCK, BLOCK)
    shaped = jnp.where(block_rows[None, :, None, :, None], shaped, -1e30)
    return shaped.reshape(heads, rows, cols)


def body(queries, key_rows, value_rows, block_mask):
    frame_count = lax.axis_size("frame")
    frame_id = lax.axis_index("frame")
    width_local = queries.shape[1] // lax.axis_size("head")
    head_count = width_local // HDIM
    frame_len = BF * BLOCK
    score_scale = 1.0 / math.sqrt(HDIM)
    query_frame, key_frame, value_frame = (
        lax.all_to_all(queries, "head", split_axis=1, concat_axis=0, tiled=True),
        lax.all_to_all(key_rows, "head", split_axis=1, concat_axis=0, tiled=True),
        lax.all_to_all(value_rows, "head", split_axis=1, concat_axis=0, tiled=True),
    )
    paired = jnp.concatenate([key_frame, value_frame], axis=1)
    beside = padded(paired, (("frame", 0),), frame_len)
    mask_grid = block_mask.reshape(frame_count, BF, frame_count, BF)
    block_ids = jnp.arange(BF, dtype=jnp.int32)
    towards = lax.dynamic_index_in_dim(mask_grid, frame_id, 2, keepdims=False)
    outgoing = jnp.minimum(jnp.sum(jnp.max(towards, axis=1) * block_ids[None, :], axis=1), BF - 1)
    blocks = paired.reshape(BF, BLOCK, 2 * width_local)
    parcel = jnp.take(blocks, outgoing, axis=0)
    distant_kv = lax.all_to_all(parcel, "frame", split_axis=0, concat_axis=0, tiled=True).reshape(
        frame_count * BLOCK, 2 * width_local
    )
    own_rows = lax.dynamic_index_in_dim(mask_grid, frame_id, 0, keepdims=False)
    incoming = jnp.minimum(jnp.sum(jnp.max(own_rows, axis=0) * block_ids[None, :], axis=1), BF - 1)
    padded_rows = jnp.pad(own_rows, ((0, 0), (1, 1), (0, 0)))
    near_mask = lax.dynamic_slice_in_dim(padded_rows, frame_id, 3, 1).reshape(BF, 3 * BF)
    match = (block_ids[None, None, :] == incoming[None, :, None]).astype(jnp.int32)
    far_mask = jnp.sum(own_rows * match, axis=2)
    frame_ids = jnp.arange(frame_count, dtype=jnp.int32)
    distant = (jnp.abs(frame_ids - frame_id) >= 2).astype(jnp.int32)
    far_mask = far_mask * distant[None, :]
    near_on = near_mask > 0
    far_on = far_mask > 0
    joint_on = jnp.concatenate([near_on, far_on], axis=1)
    near_keys = beside[:, :width_local].reshape(3 * frame_len, head_count, HDIM)
    near_values = beside[:, width_local:].reshape(3 * frame_len, head_count, HDIM)
    far_keys = distant_kv[:, :width_local].reshape(frame_count * BLOCK, head_count, HDIM)
    far_values = distant_kv[:, width_local:].reshape(frame_count * BLOCK, head_count, HDIM)
    all_keys = jnp.concatenate([near_keys, far_keys], axis=0)
    all_values = jnp.concatenate([near_values, far_values], axis=0)
    query_heads = query_frame.reshape(frame_len, head_count, HDIM)
    step_blocks = math.gcd(BF, max(1, 256 // BLOCK))
    row_step = step_blocks * BLOCK

    def one_step(step_no):
        row_start = step_no * row_step
        block_start = step_no * step_blocks
        query_part = lax.dynamic_slice_in_dim(query_heads, row_start, row_step, 0)
        rows_on = lax.dynamic_slice_in_dim(joint_on, block_start, step_blocks, 0)
        scores = masked_scores(query_part, all_keys, rows_on, score_scale)
        row_top = jnp.max(scores, axis=2, keepdims=True)
        weights = jnp.exp(scores - row_top)
        denominator = jnp.sum(weights, axis=2)
        summed = jnp.einsum(
            "htu,uhd->thd",
            weights.astype(jnp.bfloat16),
            all_values,
            preferred_element_type=jnp.float32,
        )
        scaled = summed / jnp.transpose(denominator)[:, :, None]
        return scaled.astype(jnp.bfloat16).reshape(row_step, width_local)

    stacked = lax.map(one_step, jnp.arange(BF // step_blocks, dtype=jnp.int32))
    result = stacked.reshape(frame_len, width_local)
    return lax.all_to_all(result, "head", split_axis=0, concat_axis=1, tiled=True)


def solution(mesh):
    placed = (
        P(("frame", "head"), None),
        P(("frame", "head"), None),
        P(("frame", "head"), None),
        P(),
    )
    return jax.shard_map(
        body, mesh=mesh, in_specs=placed, out_specs=P(("frame", "head"), None), check_vma=False
    )
```

profile of v0, /device:TPU:16, one launch (start us, length us, event | category | flops | bytes accessed | tf_op | source)
XLA Modules:
  0.0 957.5 jit_solution(16311673494765231983)
XLA Ops:
  0.0 4.7 copy.96
  4.7 3.9 all-to-all-start.1
  8.6 4.7 copy.98
  13.3 31.6 %all-to-all-done.1 = bf16[512,2,1536]{0,2,1:T(8,128)(2,1)S(1)} async-done(((bf16[512,2,1536]{0,2,1:T(8,128)(2,1)}), bf16[512,2,1536]{0,2,1:T(8,128)(2,1)S(1)}, u32[]{:S(2)}, u32[]{:S(2)}) %all-to-all-start.1) | async-done | bytes 3145760 | tf_op jit(solution)/shard_map/all_to_all | solution.py:46
  45.0 5.2 all-to-all-start.2
  50.2 1.6 reshape.114
  51.7 4.6 copy.94
  56.4 1.2 dynamic-slice_reduce_fusion
  57.7 3.2 copy.97
  60.9 24.8 %all-to-all-done.2 = bf16[512,2,1536]{0,2,1:T(8,128)(2,1)} async-done(((bf16[512,2,1536]{0,2,1:T(8,128)(2,1)}), bf16[512,2,1536]{0,2,1:T(8,128)(2,1)}, u32[]{:S(2)}, u32[]{:S(2)}) %all-to-all-start.2) | async-done | bytes 3145760 | tf_op jit(solution)/shard_map/all_to_all | solution.py:47
  85.7 5.2 all-to-all-start
  90.9 4.7 copy.99
  95.6 5.2 pad_maximum_fusion.4
  100.8 9.2 gather_fusion
  110.1 10.9 %broadcast_select_fusion = bf16[16,128,3072]{2,1,0:T(8,128)(2,1)} fusion(bf16[16,128,3072]{2,1,0:T(8,128)(2,1)} %gather_fusion, pred[16]{0:T(512)(128)(4,1)S(1)} %compare_and_fusion), kind=kLoop, calls=%fused_computation.21 | loop fusion | flops 6291456 | bytes 25165840 | tf_op jit(solution)/shard_map/jit(_take)/select_n | solution.py:56
  121.0 4.6 all-to-all-done
  125.6 6.2 all-to-all-start.3
  131.8 5.3 pad_maximum_fusion.3
  137.0 2.0 collective-permute-start
  139.1 4.4 collective-permute-start.1
  143.5 0.9 dynamic-slice_reduce_fusion.1
  144.6 1.1 multiply_reduce_fusion
  145.8 7.9 copy.95
  153.8 6.2 reshape.115
  159.9 311.8 %collective-permute-done = bf16[1024,3072]{1,0:T(8,128)(2,1)} collective-permute-done((bf16[1024,3072]{1,0:T(8,128)(2,1)}, bf16[1024,3072]{1,0:T(8,128)(2,1)}, u32[]{:S(2)}, u32[]{:S(2)}) %collective-permute-start) | collective-permute-done | bytes 6291488 | tf_op jit(solution)/shard_map/ppermute | solution.py:20
  471.7 14.9 %pad_maximum_fusion = bf16[3072,3072]{1,0:T(8,128)(2,1)} fusion(bf16[1024,3072]{1,0:T(8,128)(2,1)} %collective-permute-done.1, bf16[1024,1536]{1,0:T(8,128)(2,1)} %bitcast.69, bf16[1024,1536]{1,0:T(8,128)(2,1)S(1)} %bitcast.66, bf16[1024,3072]{1,0:T(8,128)(2,1)} %collective-permute-done), kind=kLoop, calls=%fused_computation.18 | loop fusion | flops 75497472 | bytes 37748736 | tf_op jit(solution)/shard_map/concatenate | solution.py:22
  486.6 14.6 %fusion.17 = (bf16[3072,1536]{1,0:T(8,128)(2,1)}, bf16[3072,1536]{1,0:T(8,128)(2,1)}) fusion(bf16[3072,3072]{1,0:T(8,128)(2,1)} %pad_maximum_fusion), kind=kLoop, calls=%fused_computation.43 | loop fusion | bytes 37748736 | tf_op jit(solution)/shard_map/slice | solution.py:73
  501.2 12.6 %copy.105 = bf16[3072,1536]{0,1:T(8,128)(2,1)} copy(bf16[3072,1536]{1,0:T(8,128)(2,1)} %get-tuple-element.110) | data formatting | bytes 18874368 | tf_op jit(solution)/shard_map/slice | solution.py:73
  513.9 12.6 %copy.100 = bf16[3072,1536]{0,1:T(8,128)(2,1)} copy(bf16[3072,1536]{1,0:T(8,128)(2,1)} %get-tuple-element.111) | data formatting | bytes 18874368 | tf_op jit(solution)/shard_map/slice | solution.py:72
  526.5 10.2 %fusion.18 = (bf16[2048,1536]{1,0:T(8,128)(2,1)}, bf16[2048,1536]{1,0:T(8,128)(2,1)}) fusion(bf16[2048,3072]{1,0:T(8,128)(2,1)} %bitcast.19), kind=kLoop, calls=%fused_computation.44 | loop fusion | bytes 25165824 | tf_op jit(solution)/shard_map/slice | solution.py:75
  536.7 8.7 copy.106
  545.4 8.8 copy.117
  554.2 13.1 %pad_maximum_fusion.1 = bf16[5120,12,128]{0,2,1:T(8,128)(2,1)} fusion(bf16[2048,12,128]{0,2,1:T(8,128)(2,1)} %bitcast.73, bf16[3072,12,128]{0,2,1:T(8,128)(2,1)} %bitcast.71), kind=kLoop, calls=%fused_computation.19 | loop fusion | flops 31457280 | bytes 31457280 | tf_op jit(solution)/shard_map/concatenate | solution.py:76
  567.3 20.6 %copy.108 = bf16[5120,12,128]{2,0,1:T(8,128)(2,1)} copy(bf16[5120,12,128]{0,2,1:T(8,128)(2,1)} %pad_maximum_fusion.1) | data formatting | bytes 31457280 | tf_op jit(solution)/shard_map/while | solution.py:100
  587.9 13.1 %pad_maximum_fusion.2 = bf16[5120,12,128]{0,2,1:T(8,128)(2,1)} fusion(bf16[2048,12,128]{0,2,1:T(8,128)(2,1)} %bitcast.72, bf16[3072,12,128]{0,2,1:T(8,128)(2,1)} %bitcast.70), kind=kLoop, calls=%fused_computation.20 | loop fusion | flops 31457280 | bytes 31457280 | tf_op jit(solution)/shard_map/concatenate | solution.py:77
  601.0 324.5 %while.10 = (s32[]{:T(128)}, bf16[4,256,1536]{2,1,0:T(8,128)(2,1)}, s32[4]{0:T(128)S(1)}, pred[8,40]{1,0:T(8,128)(4,1)S(1)}, bf16[1024,12,128]{0,2,1:T(8,128)(2,...) while((s32[]{:T(128)}, bf16[4,256,1536]{2,1,0:T(8,128)(2,1)}, ...), condition=%wide.region_8.9_spmd, body=%wide.region_5.8_spmd.sunk | while | flops 8226859008 | bytes 232846288 | solution.py:100
  601.0 0.7 dynamic_slice.41
  602.3 0.4 broadcast_in_dim.73
  602.8 0.6 copy.123
  604.1 28.4 %fusion.30 = (f32[12,256]{1,0:T(8,128)S(1)}, f32[12,256,5120]{2,1,0:T(8,128)}) fusion(pred[256,5120]{1,0:T(8,128)(4,1)S(1)} %bitcast.60, bf16[5120,12,128]{2,0,1:T(8,128)(2,1)} %get-tuple-element.192, bf16[1024,12,128]{0,2,1:T(8,128)(2,1)} %get-tuple-element.191, s32[]{:T(128)S(6)} %select_n.73), kind=kOutput, calls=%fused_computation.3.clone.1 | convolution fusion | flops 4073714688 | bytes 80752640 | tf_op jit(solution)/shard_map/while/body/eval_jaxpr/thd,uhd->htu/dot_general | solution.py:28
  632.5 20.6 %fusion.31 = f32[12,256]{1,0:T(8,128)S(1)} fusion(f32[12,256,5120]{2,1,0:T(8,128)} %get-tuple-element.159, f32[12,256]{1,0:T(8,128)S(1)} %get-tuple-element.160, pred[256,5120]{1,0:T(8,128)(4,1)S(1)} %bitcast.61), kind=kLoop, calls=%fused_computation.4.clone.1 | loop fusion | flops 62911488 | bytes 64249856 | tf_op jit(solution)/shard_map/while/body/eval_jaxpr/reduce_sum | solution.py:90
  653.1 27.8 %fusion.32 = bf16[256,12,128]{0,2,1:T(8,128)(2,1)S(1)} fusion(bf16[5120,12,128]{0,2,1:T(8,128)(2,1)} %get-tuple-element.193, f32[12,256,5120]{2,1,0:T(8,128)} %get-tuple-element.159, f32[12,256]{1,0:T(8,128)S(1)} %get-tuple-element.160, pred[256,5120]{1,0:T(8,128)(4,1)S(1)} %bitcast.62, f32[256,12]{0,1:T(8,128)S(1)} %bitcast.82), kind=kOutput, calls=%fused_computation.10.clone.1 | convolution fusion | flops 4090232832 | bytes 80764928 | tf_op jit(solution)/shard_map/while/body/eval_jaxpr/htu,uhd->thd/dot_general | solution.py:91
  681.1 0.9 constant_dynamic-update-slice_fusion.2
  682.1 0.7 dynamic_slice.41
  683.9 0.6 copy.123
  685.2 28.4 %fusion.30 = (f32[12,256]{1,0:T(8,128)S(1)}, f32[12,256,5120]{2,1,0:T(8,128)}) fusion(pred[256,5120]{1,0:T(8,128)(4,1)S(1)} %bitcast.60, bf16[5120,12,128]{2,0,1:T(8,128)(2,1)} %get-tuple-element.192, bf16[1024,12,128]{0,2,1:T(8,128)(2,1)} %get-tuple-element.191, s32[]{:T(128)S(6)} %select_n.73), kind=kOutput, calls=%fused_computation.3.clone.1 | convolution fusion | flops 4073714688 | bytes 80752640 | tf_op jit(solution)/shard_map/while/body/eval_jaxpr/thd,uhd->htu/dot_general | solution.py:28
  713.6 20.6 %fusion.31 = f32[12,256]{1,0:T(8,128)S(1)} fusion(f32[12,256,5120]{2,1,0:T(8,128)} %get-tuple-element.159, f32[12,256]{1,0:T(8,128)S(1)} %get-tuple-element.160, pred[256,5120]{1,0:T(8,128)(4,1)S(1)} %bitcast.61), kind=kLoop, calls=%fused_computation.4.clone.1 | loop fusion | flops 62911488 | bytes 64249856 | tf_op jit(solution)/shard_map/while/body/eval_jaxpr/reduce_sum | solution.py:90
  734.2 27.8 %fusion.32 = bf16[256,12,128]{0,2,1:T(8,128)(2,1)S(1)} fusion(bf16[5120,12,128]{0,2,1:T(8,128)(2,1)} %get-tuple-element.193, f32[12,256,5120]{2,1,0:T(8,128)} %get-tuple-element.159, f32[12,256]{1,0:T(8,128)S(1)} %get-tuple-element.160, pred[256,5120]{1,0:T(8,128)(4,1)S(1)} %bitcast.62, f32[256,12]{0,1:T(8,128)S(1)} %bitcast.82), kind=kOutput, calls=%fused_computation.10.clone.1 | convolution fusion | flops 4090232832 | bytes 80764928 | tf_op jit(solution)/shard_map/while/body/eval_jaxpr/htu,uhd->thd/dot_general | solution.py:91
  762.3 0.9 constant_dynamic-update-slice_fusion.2
  763.2 0.7 dynamic_slice.41
  765.0 0.6 copy.123
  766.3 28.4 %fusion.30 = (f32[12,256]{1,0:T(8,128)S(1)}, f32[12,256,5120]{2,1,0:T(8,128)}) fusion(pred[256,5120]{1,0:T(8,128)(4,1)S(1)} %bitcast.60, bf16[5120,12,128]{2,0,1:T(8,128)(2,1)} %get-tuple-element.192, bf16[1024,12,128]{0,2,1:T(8,128)(2,1)} %get-tuple-element.191, s32[]{:T(128)S(6)} %select_n.73), kind=kOutput, calls=%fused_computation.3.clone.1 | convolution fusion | flops 4073714688 | bytes 80752640 | tf_op jit(solution)/shard_map/while/body/eval_jaxpr/thd,uhd->htu/dot_general | solution.py:28
  794.8 20.6 %fusion.31 = f32[12,256]{1,0:T(8,128)S(1)} fusion(f32[12,256,5120]{2,1,0:T(8,128)} %get-tuple-element.159, f32[12,256]{1,0:T(8,128)S(1)} %get-tuple-element.160, pred[256,5120]{1,0:T(8,128)(4,1)S(1)} %bitcast.61), kind=kLoop, calls=%fused_computation.4.clone.1 | loop fusion | flops 62911488 | bytes 64249856 | tf_op jit(solution)/shard_map/while/body/eval_jaxpr/reduce_sum | solution.py:90
  815.3 27.8 %fusion.32 = bf16[256,12,128]{0,2,1:T(8,128)(2,1)S(1)} fusion(bf16[5120,12,128]{0,2,1:T(8,128)(2,1)} %get-tuple-element.193, f32[12,256,5120]{2,1,0:T(8,128)} %get-tuple-element.159, f32[12,256]{1,0:T(8,128)S(1)} %get-tuple-element.160, pred[256,5120]{1,0:T(8,128)(4,1)S(1)} %bitcast.62, f32[256,12]{0,1:T(8,128)S(1)} %bitcast.82), kind=kOutput, calls=%fused_computation.10.clone.1 | convolution fusion | flops 4090232832 | bytes 80764928 | tf_op jit(solution)/shard_map/while/body/eval_jaxpr/htu,uhd->thd/dot_general | solution.py:91
  843.4 0.9 constant_dynamic-update-slice_fusion.2
  844.3 0.7 dynamic_slice.41
  846.1 0.6 copy.123
  847.4 28.4 %fusion.30 = (f32[12,256]{1,0:T(8,128)S(1)}, f32[12,256,5120]{2,1,0:T(8,128)}) fusion(pred[256,5120]{1,0:T(8,128)(4,1)S(1)} %bitcast.60, bf16[5120,12,128]{2,0,1:T(8,128)(2,1)} %get-tuple-element.192, bf16[1024,12,128]{0,2,1:T(8,128)(2,1)} %get-tuple-element.191, s32[]{:T(128)S(6)} %select_n.73), kind=kOutput, calls=%fused_computation.3.clone.1 | convolution fusion | flops 4073714688 | bytes 80752640 | tf_op jit(solution)/shard_map/while/body/eval_jaxpr/thd,uhd->htu/dot_general | solution.py:28
  875.9 20.6 %fusion.31 = f32[12,256]{1,0:T(8,128)S(1)} fusion(f32[12,256,5120]{2,1,0:T(8,128)} %get-tuple-element.159, f32[12,256]{1,0:T(8,128)S(1)} %get-tuple-element.160, pred[256,5120]{1,0:T(8,128)(4,1)S(1)} %bitcast.61), kind=kLoop, calls=%fused_computation.4.clone.1 | loop fusion | flops 62911488 | bytes 64249856 | tf_op jit(solution)/shard_map/while/body/eval_jaxpr/reduce_sum | solution.py:90
  896.4 27.8 %fusion.32 = bf16[256,12,128]{0,2,1:T(8,128)(2,1)S(1)} fusion(bf16[5120,12,128]{0,2,1:T(8,128)(2,1)} %get-tuple-element.193, f32[12,256,5120]{2,1,0:T(8,128)} %get-tuple-element.159, f32[12,256]{1,0:T(8,128)S(1)} %get-tuple-element.160, pred[256,5120]{1,0:T(8,128)(4,1)S(1)} %bitcast.62, f32[256,12]{0,1:T(8,128)S(1)} %bitcast.82), kind=kOutput, calls=%fused_computation.10.clone.1 | convolution fusion | flops 4090232832 | bytes 80764928 | tf_op jit(solution)/shard_map/while/body/eval_jaxpr/htu,uhd->thd/dot_general | solution.py:91
  924.5 0.9 constant_dynamic-update-slice_fusion.2
  925.4 24.6 %all_to_all.78 = bf16[2,512,1536]{2,1,0:T(8,128)(2,1)S(1)} all-to-all(bf16[2,512,1536]{2,1,0:T(8,128)(2,1)} %bitcast.81), channel_id=1, replica_groups=mesh['frame'=16,'head'=2] {'head'}, dimensions={0} | all-to-all | bytes 6291456 | tf_op jit(solution)/shard_map/all_to_all | solution.py:102
  950.0 2.8 copy.110
  952.8 4.6 copy.111
  (31 shorter events, 2.9 us)
Async XLA Ops:
  0.0 50.2 %copy-start.1 = (s32[128,128]{1,0:T(8,128)S(1)}, s32[128,128]{1,0:T(8,128)}, u32[]{:S(2)}) copy-start(s32[128,128]{1,0:T(8,128)} %param.9) | copy-start | bytes 196612
  4.7 40.3 %all-to-all-start.1 = ((bf16[512,2,1536]{0,2,1:T(8,128)(2,1)}), bf16[512,2,1536]{0,2,1:T(8,128)(2,1)S(1)}, u32[]{:S(2)}, u32[]{:S(2)}) async-start(bf16[512,2,1536]{0,2,1:T(8,128)(2,1)} %bitcast.78), calls=%async_computation.1 | async-start | bytes 6291456 | tf_op jit(solution)/shard_map/all_to_all | solution.py:46
  45.0 12.7 %copy-start = (bf16[512,2,1536]{0,2,1:T(8,128)(2,1)}, bf16[512,2,1536]{0,2,1:T(8,128)(2,1)S(1)}, u32[]{:S(2)}) copy-start(bf16[512,2,1536]{0,2,1:T(8,128)(2,1)S(1)} %all-to-all-done.1) | copy-start | bytes 9437188
  45.0 40.8 %all-to-all-start.2 = ((bf16[512,2,1536]{0,2,1:T(8,128)(2,1)}), bf16[512,2,1536]{0,2,1:T(8,128)(2,1)}, u32[]{:S(2)}, u32[]{:S(2)}) async-start(bf16[512,2,1536]{0,2,1:T(8,128)(2,1)} %bitcast.76), calls=%async_computation.2 | async-start | bytes 6291456 | tf_op jit(solution)/shard_map/all_to_all | solution.py:47
  85.7 39.8 %all-to-all-start = ((bf16[512,2,1536]{0,2,1:T(8,128)(2,1)}), bf16[512,2,1536]{0,2,1:T(8,128)(2,1)}, u32[]{:S(2)}, u32[]{:S(2)}) async-start(bf16[512,2,1536]{0,2,1:T(8,128)(2,1)} %bitcast.77), calls=%async_computation | async-start | bytes 6291456 | tf_op jit(solution)/shard_map/all_to_all | solution.py:45
  125.6 400.9 %all-to-all-start.3 = ((bf16[16,128,3072]{2,1,0:T(8,128)(2,1)}), bf16[16,128,3072]{2,1,0:T(8,128)(2,1)}, u32[]{:S(2)}, u32[]{:S(2)}) async-start(bf16[16,128,3072]{2,1,0:T(8,128)(2,1)} %broadcast_select_fusion), calls=%async_computation.3 | async-start | bytes 25165824 | tf_op jit(solution)/shard_map/all_to_all | solution.py:57
  137.0 334.7 %collective-permute-start = (bf16[1024,3072]{1,0:T(8,128)(2,1)}, bf16[1024,3072]{1,0:T(8,128)(2,1)}, u32[]{:S(2)}, u32[]{:S(2)}) collective-permute-start(bf16[1024,3072]{1,0:T(8,128)(2,1)} %pad_maximum_fusion.3), channel_id=1, source_target_pairs={{0,2},{2,4},{4,6},{6,8},{8,10},{10,12},{12,14},{14,16},{16,18},{18... | collective-permute-start | bytes 18874376 | tf_op jit(solution)/shard_map/ppermute | solution.py:20
  139.1 332.6 %collective-permute-start.1 = (bf16[1024,3072]{1,0:T(8,128)(2,1)}, bf16[1024,3072]{1,0:T(8,128)(2,1)}, u32[]{:S(2)}, u32[]{:S(2)}) collective-permute-start(bf16[1024,3072]{1,0:T(8,128)(2,1)} %pad_maximum_fusion.3), channel_id=1, source_target_pairs={{2,0},{4,2},{6,4},{8,6},{10,8},{12,10},{14,12},{16,14},{18,16},{20... | collective-permute-start | bytes 18874376 | tf_op jit(solution)/shard_map/ppermute | solution.py:21
where the time goes:
time: 961 us; the launch traced here: 957 us
  waiting for transfers between devices  373 us (39%)
  matrix products  225 us (23%)
  local copies, waits for them, and re-layouts  154 us (16%)
  other arithmetic  148 us (15%)
  starting transfers between devices  27 us (3%)
  blocking collectives  24.6 us (3%)
    ppermute x1, waiting for transfers between devices, padded(): before = lax.ppermute(last, axis, up)  312 us
    dot_general x4, matrix products, masked_scores(): jnp.einsum('thd,uhd->htu', query_part, key_part, preferred_element_type=j...  114 us
    dot_general x4, matrix products, one_step(): jnp.einsum('htu,uhd->thd', weights.astype(jnp.bfloat16), all_values, pref...  111 us
    reduce_sum x4, other arithmetic, one_step(): denominator = jnp.sum(weights, axis=2)  82.2 us
    all_to_all x1, waiting for transfers between devices, body(): lax.all_to_all(key_rows, 'head', split_axis=1, concat_axis=0, tiled=True)  31.6 us
    slice x2, local copies, waits for them, and re-layouts, body(): beside[:, width_local:].reshape(3 * frame_len, head_count, HDIM)  27.2 us
    all_to_all x1, waiting for transfers between devices, body(): lax.all_to_all(value_rows, 'head', split_axis=1, concat_axis=0, tiled=True)  24.8 us
    all_to_all x1, blocking collectives, body(): lax.all_to_all(result, 'head', split_axis=0, concat_axis=1, tiled=True)  24.6 us
  transfers between devices with their start and end apart: 6, of which 4 were waited for; matrix products, arithmetic and copies ran while one was open for 13% of the time, Pallas kernels for 0%

commit v1 on v0

v1 whole, which is shorter than its diff:
```python
import functools
import math

import jax
import jax.numpy as jnp
from jax import lax
from jax.experimental import pallas as pl
from jax.experimental.pallas import tpu as pltpu
from jax.sharding import PartitionSpec as P

HDIM = 128
BLOCK = 128
BF = 8
MESH = pl.DeviceIdType.MESH
GROUP_HEADS = 2
TILE_BLOCKS = 2
LOG2E = 1.4426950408889634


def kernel(
    frames,
    heads_axis,
    groups,
    pick_ref,
    bias_ref,
    q_ref,
    k_ref,
    v_ref,
    out_ref,
    own,
    near,
    far,
    parcel,
    stage,
    rows,
    local_sem,
    swap_send,
    swap_recv,
    near_send,
    near_recv,
    far_send,
    far_recv,
    out_local,
    out_send,
    out_recv,
):
    f = lax.axis_index("frame")
    h = lax.axis_index("head")
    span = GROUP_HEADS * HDIM
    nb = BF // heads_axis
    sources = (k_ref, v_ref, q_ref)

    def columns(owner, g):
        return pl.ds(pl.multiple_of((owner * groups + g) * span, span), span)

    def landing(kind, g, part):
        place = pl.ds(part * nb, nb)
        return rows.at[g, place] if kind == 2 else own.at[g, kind, place]

    def swap(kind, g, shift):
        to = lax.rem(h + shift, heads_axis)
        return pltpu.make_async_remote_copy(
            src_ref=sources[kind].at[:, :, columns(to, g)],
            dst_ref=landing(kind, g, h),
            send_sem=swap_send.at[kind, g, shift - 1],
            recv_sem=swap_recv.at[kind, g, shift - 1],
            device_id=(f, to),
            device_id_type=MESH,
        )

    def swap_wait(kind, g, shift):
        start = lax.rem(h + heads_axis - shift, heads_axis)
        pltpu.make_async_remote_copy(
            src_ref=sources[kind].at[:, :, columns(h, g)],
            dst_ref=landing(kind, g, start),
            send_sem=swap_send.at[kind, g, shift - 1],
            recv_sem=swap_recv.at[kind, g, shift - 1],
            device_id=(f, start),
            device_id_type=MESH,
        ).wait_recv()

    def keep(kind, g):
        return pltpu.make_async_copy(
            sources[kind].at[:, :, columns(h, g)], landing(kind, g, h), local_sem.at[kind, g]
        )

    def near_copy(g, side):
        to = f + 1 if side == 0 else f - 1
        return pltpu.make_async_remote_copy(
            src_ref=own.at[g],
            dst_ref=near.at[g, side],
            send_sem=near_send.at[g, side],
            recv_sem=near_recv.at[g, side],
            device_id=(to, h),
            device_id_type=MESH,
        )

    def far_copy(g, to):
        return pltpu.make_async_remote_copy(
            src_ref=parcel.at[g, to],
            dst_ref=far.at[g, f],
            send_sem=far_send.at[g, to],
            recv_sem=far_recv.at[g, f],
            device_id=(to, h),
            device_id_type=MESH,
        )

    def far_wait(g, start):
        pltpu.make_async_remote_copy(
            src_ref=parcel.at[g, start],
            dst_ref=far.at[g, start],
            send_sem=far_send.at[g, start],
            recv_sem=far_recv.at[g, start],
            device_id=(start, h),
            device_id_type=MESH,
        ).wait_recv()

    def distant(other):
        return (other - f >= 2) | (f - other >= 2)

    def out_copy(g, shift):
        to = lax.rem(h + shift, heads_axis)
        return pltpu.make_async_remote_copy(
            src_ref=rows.at[g, pl.ds(to * nb, nb)],
            dst_ref=out_ref.at[:, :, columns(h, g)],
            send_sem=out_send.at[g, shift - 1],
            recv_sem=out_recv.at[g, shift - 1],
            device_id=(f, to),
            device_id_type=MESH,
        )

    def out_wait(g, shift):
        start = lax.rem(h + heads_axis - shift, heads_axis)
        pltpu.make_async_remote_copy(
            src_ref=rows.at[g, pl.ds(start * nb, nb)],
            dst_ref=out_ref.at[:, :, columns(start, g)],
            send_sem=out_send.at[g, shift - 1],
            recv_sem=out_recv.at[g, shift - 1],
            device_id=(f, start),
            device_id_type=MESH,
        ).wait_recv()

    def out_keep(g):
        return pltpu.make_async_copy(
            rows.at[g, pl.ds(h * nb, nb)], out_ref.at[:, :, columns(h, g)], out_local.at[g]
        )

    barrier = pltpu.get_barrier_semaphore()

    @pl.loop(1, frames)
    def _(step):
        pl.semaphore_signal(
            barrier, inc=1, device_id=(lax.rem(f + step, frames), h), device_id_type=MESH
        )

    for shift in range(1, heads_axis):
        pl.semaphore_signal(
            barrier,
            inc=1,
            device_id=(f, lax.rem(h + shift, heads_axis)),
            device_id_type=MESH,
        )
    pl.semaphore_wait(barrier, frames - 1 + heads_axis - 1)

    @pl.loop(0, groups)
    def _(g):
        for kind in (0, 1):
            for shift in range(1, heads_axis):
                swap(kind, g, shift).start()
            keep(kind, g).start()

    @pl.loop(0, groups)
    def _(g):
        for shift in range(1, heads_axis):
            swap(2, g, shift).start()
        keep(2, g).start()

    @pl.loop(0, groups)
    def _(g):
        @pl.loop(0, frames)
        def _(other):
            @pl.when(jnp.logical_not(distant(other)))
            def _():
                far[g, other] = jnp.zeros(far.shape[2:], far.dtype)

        @pl.when(f == 0)
        def _():
            near[g, 0] = jnp.zeros(near.shape[2:], near.dtype)

        @pl.when(f == frames - 1)
        def _():
            near[g, 1] = jnp.zeros(near.shape[2:], near.dtype)

    @pl.loop(0, groups)
    def _(g):
        for kind in (0, 1):
            keep(kind, g).wait()
            for shift in range(1, heads_axis):
                swap_wait(kind, g, shift)
            stage[kind] = own[g, kind]

        @pl.loop(1, frames)
        def _(step):
            to = lax.rem(f + step, frames)

            @pl.when(distant(to))
            def _():
                block = pick_ref[to]
                parcel[g, to, 0] = stage[0, block]
                parcel[g, to, 1] = stage[1, block]
                far_copy(g, to).start()

        @pl.when(f < frames - 1)
        def _():
            near_copy(g, 0).start()

        @pl.when(f > 0)
        def _():
            near_copy(g, 1).start()

    scale = LOG2E / math.sqrt(HDIM)
    frame_len = BF * BLOCK
    tile = TILE_BLOCKS * BLOCK

    @pl.loop(0, groups)
    def _(g):
        keep(2, g).wait()
        for shift in range(1, heads_axis):
            swap_wait(2, g, shift)

        @pl.when(f > 0)
        def _():
            near_copy(g, 0).wait_recv()

        @pl.when(f < frames - 1)
        def _():
            near_copy(g, 1).wait_recv()

        @pl.loop(1, frames)
        def _(step):
            start = lax.rem(f + step, frames)

            @pl.when(distant(start))
            def _():
                far_wait(g, start)

        @pl.loop(0, BF // TILE_BLOCKS)
        def _(t):
            for head in range(GROUP_HEADS):
                lanes = slice(head * HDIM, (head + 1) * HDIM)
                query = rows[g, pl.ds(t * TILE_BLOCKS, TILE_BLOCKS), :, lanes].reshape(tile, HDIM)

                def part(which, no):
                    if no == 0:
                        held = own[g, which, :, :, lanes]
                    elif no < 3:
                        held = near[g, no - 1, which, :, :, lanes]
                    else:
                        held = far[g, pl.ds((no - 3) * BF, BF), which, :, lanes]
                    return held.reshape(frame_len, HDIM)

                count = 3 + frames // BF
                scores = []
                top = None
                for no in range(count):
                    s = lax.dot_general(
                        query,
                        part(0, no),
                        (((1,), (1,)), ((), ())),
                        preferred_element_type=jnp.float32,
                    )
                    off = bias_ref[t, :, :, no * frame_len : (no + 1) * frame_len]
                    s = (s.reshape(TILE_BLOCKS, BLOCK, frame_len) + off).reshape(tile, frame_len)
                    part_top = jnp.max(s, axis=1, keepdims=True)
                    top = part_top if top is None else jnp.maximum(top, part_top)
                    scores.append(s)
                total = None
                summed = None
                for no in range(count):
                    weights = jnp.exp2((scores[no] - top) * scale)
                    part_total = jnp.sum(weights, axis=1, keepdims=True)
                    part_sum = jnp.dot(
                        weights.astype(jnp.bfloat16),
                        part(1, no),
                        preferred_element_type=jnp.float32,
                    )
                    total = part_total if total is None else total + part_total
                    summed = part_sum if summed is None else summed + part_sum
                result = (summed / total).astype(jnp.bfloat16)
                rows[g, pl.ds(t * TILE_BLOCKS, TILE_BLOCKS), :, lanes] = result.reshape(
                    TILE_BLOCKS, BLOCK, HDIM
                )

        for shift in range(1, heads_axis):
            out_copy(g, shift).start()
        out_keep(g).start()

    @pl.loop(0, groups)
    def _(g):
        for kind in range(3):
            for shift in range(1, heads_axis):
                swap(kind, g, shift).wait_send()

        @pl.when(f < frames - 1)
        def _():
            near_copy(g, 0).wait_send()

        @pl.when(f > 0)
        def _():
            near_copy(g, 1).wait_send()

        @pl.loop(1, frames)
        def _(step):
            to = lax.rem(f + step, frames)

            @pl.when(distant(to))
            def _():
                far_copy(g, to).wait_send()

        out_keep(g).wait()
        for shift in range(1, heads_axis):
            out_copy(g, shift).wait_send()
            out_wait(g, shift)


def body(queries, key_rows, value_rows, block_mask):
    frames = lax.axis_size("frame")
    heads_axis = lax.axis_size("head")
    frame_id = lax.axis_index("frame")
    local, width = queries.shape
    nb = local // BLOCK
    span = GROUP_HEADS * HDIM
    groups = width // heads_axis // span
    mask_grid = block_mask.reshape(frames, BF, frames, BF)
    block_ids = jnp.arange(BF, dtype=jnp.int32)
    towards = lax.dynamic_index_in_dim(mask_grid, frame_id, 2, keepdims=False)
    pick = jnp.minimum(jnp.sum(jnp.max(towards, axis=1) * block_ids[None, :], axis=1), BF - 1)
    own_rows = lax.dynamic_index_in_dim(mask_grid, frame_id, 0, keepdims=False)
    padded_rows = jnp.pad(own_rows, ((0, 0), (1, 1), (0, 0)))
    near_mask = lax.dynamic_slice_in_dim(padded_rows, frame_id, 3, 1)
    frame_ids = jnp.arange(frames, dtype=jnp.int32)
    distant = jnp.abs(frame_ids - frame_id) >= 2
    far_mask = jnp.max(own_rows, axis=2) * distant[None, :].astype(jnp.int32)
    joint = jnp.concatenate([near_mask[:, 1], near_mask[:, 0], near_mask[:, 2], far_mask], axis=1)
    bias = jnp.where(jnp.repeat(joint > 0, BLOCK, axis=1), 0.0, -1e30).astype(jnp.float32)
    bias = bias.reshape(BF // TILE_BLOCKS, TILE_BLOCKS, 1, bias.shape[1])
    folded = (nb, BLOCK, width)
    dma = pltpu.SemaphoreType.DMA
    turns = max(heads_axis - 1, 1)
    out = pl.pallas_call(
        functools.partial(kernel, frames, heads_axis, groups),
        out_shape=jax.ShapeDtypeStruct(folded, jnp.bfloat16),
        in_specs=[
            pl.BlockSpec(memory_space=pltpu.SMEM),
            pl.BlockSpec(memory_space=pltpu.VMEM),
            pl.BlockSpec(memory_space=pl.ANY),
            pl.BlockSpec(memory_space=pl.ANY),
            pl.BlockSpec(memory_space=pl.ANY),
        ],
        out_specs=pl.BlockSpec(memory_space=pl.ANY),
        scratch_shapes=[
            pltpu.VMEM((groups, 2, BF, BLOCK, span), jnp.bfloat16),
            pltpu.VMEM((groups, 2, 2, BF, BLOCK, span), jnp.bfloat16),
            pltpu.VMEM((groups, frames, 2, BLOCK, span), jnp.bfloat16),
            pltpu.VMEM((groups, frames, 2, BLOCK, span), jnp.bfloat16),
            pltpu.VMEM((2, BF, BLOCK, span), jnp.bfloat16),
            pltpu.VMEM((groups, BF, BLOCK, span), jnp.bfloat16),
            dma((3, groups)),
            dma((3, groups, turns)),
            dma((3, groups, turns)),
            dma((groups, 2)),
            dma((groups, 2)),
            dma((groups, frames)),
            dma((groups, frames)),
            dma((groups,)),
            dma((groups, turns)),
            dma((groups, turns)),
        ],
        compiler_params=pltpu.CompilerParams(
            collective_id=0, has_side_effects=True, vmem_limit_bytes=60 * 1024 * 1024
        ),
        cost_estimate=pl.CostEstimate(
            flops=4 * BF * BLOCK * bias.shape[-1] * (width // heads_axis),
            bytes_accessed=8 * local * width,
            transcendentals=BF * BLOCK * bias.shape[-1] * groups * GROUP_HEADS,
        ),
    )(
        pick.astype(jnp.int32),
        bias,
        queries.reshape(folded),
        key_rows.reshape(folded),
        value_rows.reshape(folded),
    )
    return out.reshape(local, width)


def solution(mesh):
    placed = (
        P(("frame", "head"), None),
        P(("frame", "head"), None),
        P(("frame", "head"), None),
        P(),
    )
    return jax.shard_map(
        body, mesh=mesh, in_specs=placed, out_specs=P(("frame", "head"), None), check_vma=False
    )
```

time: 961 us -> 383 us (0.40)
  Pallas kernels: 0 us -> 374 us
  waiting for transfers between devices: 373 us -> 0 us
  matrix products: 225 us -> 0 us
  local copies, waits for them, and re-layouts: 154 us -> 6.59 us
  other arithmetic: 148 us -> 1.04 us
  starting transfers between devices: 27 us -> 0 us
  blocking collectives: 24.6 us -> 0 us
    pallas_call x0 -> x1, Pallas kernels: none -> 374 us  [body(): pl.pallas_call(functools.partial(kernel, frames, heads_axis, groups), out...]
    ppermute x2 -> x0, waiting for transfers between devices: 312 us -> none  [the longest x1 312 us: padded(): before = lax.ppermute(last, axis, up)]
    dot_general x8 -> x0, matrix products: 225 us -> none  [the longest x4 114 us: masked_scores(): jnp.einsum('thd,uhd->htu', query_part, key_part, preferred_element_type=j...]
    reduce_sum x6 -> x0, other arithmetic: 83.4 us -> none  [the longest x4 82.2 us: one_step(): denominator = jnp.sum(weights, axis=2)]
    all_to_all x4 -> x0, waiting for transfers between devices: 61 us -> none  [the longest x1 31.6 us: body(): lax.all_to_all(key_rows, 'head', split_axis=1, concat_axis=0, tiled=True)]
    slice x5 -> x1, local copies, waits for them, and re-layouts: 58.8 us -> 0.57 us  [body(): near_mask[:, 1]]
    concatenate x6 -> x0, other arithmetic: 51.6 us -> none  [the longest x1 14.9 us: padded(): value = jnp.concatenate([before, value, after], axis=dim)]
    all_to_all x1 -> x0, blocking collectives: 24.6 us -> none  [body(): lax.all_to_all(result, 'head', split_axis=0, concat_axis=1, tiled=True)]
  transfers between devices with their start and end apart: 6 -> 0, of which waited for: 4 -> 0; matrix products, arithmetic and copies ran while one was open for 13% -> 0% of each run, Pallas kernels for 0% -> 0%
where the time goes in v1:
time: 383 us; the launch traced here: 382 us
  Pallas kernels  374 us (98%)
  local copies, waits for them, and re-layouts  6.59 us (2%)
    pallas_call x1, Pallas kernels, body(): pl.pallas_call(functools.partial(kernel, frames, heads_axis, groups), out...  374 us

profile of v1, /device:TPU:16, one launch (start us, length us, event | category | flops | bytes accessed | tf_op | source)
XLA Modules:
  0.0 381.7 jit_solution(15119090222048497507)
XLA Ops:
  0.0 1.4 reshape.38
  1.4 0.1 dynamic-slice_reduce_fusion
  1.6 0.2 fusion.1
  1.8 0.1 multiply_reduce_fusion
  1.9 0.5 broadcast_minimum_fusion.pick_ref
  2.4 0.1 copy.10
  2.5 0.6 dynamic-slice_reduce_fusion.3
  3.0 0.1 fusion
  3.1 0.8 broadcast_in_dim.15
  3.9 374.0 %shard_map.46 = bf16[4,128,3072]{2,1,0:T(8,128)(2,1)} custom-call(s32[16]{0:T(128)} %broadcast_minimum_fusion.pick_ref, f32[4,2,1,5120]{3,2,1,0:T(1,128)} %bitcast.7, bf16[4,128,3072]{2,1,0:T(8,128)(2,1)} %bitcast.9, bf16[4,128,3072]{2,1,0:T(8,128)(2,1)} %bitcast.10, bf16[4,128,3072]{2,1,0:T(8,128)(2,1)} %bitcast.11), custom_call_target="tpu_custom_call" | custom-call | flops 32212254720 | bytes 12582912 | tf_op jit(solution)/shard_map/pallas_call | solution.py:350
  377.9 3.8 copy.13
  (2 shorter events, 0.0 us)

commit v2 on v1

--- a/solution.py
+++ b/solution.py
@@ -12,7 +12,7 @@
 BLOCK = 128
 BF = 8
 MESH = pl.DeviceIdType.MESH
-GROUP_HEADS = 2
+GROUP_HEADS = 1
 TILE_BLOCKS = 2
 LOG2E = 1.4426950408889634
 

time: 383 us -> 373 us (0.974)
  Pallas kernels: 374 us -> 365 us
    pallas_call x1, Pallas kernels: 374 us -> 365 us  [body(): pl.pallas_call(functools.partial(kernel, frames, heads_axis, groups), out...]
where the time goes in v2:
time: 373 us; the launch traced here: 372 us
  Pallas kernels  365 us (98%)
  local copies, waits for them, and re-layouts  6.59 us (2%)
    pallas_call x1, Pallas kernels, body(): pl.pallas_call(functools.partial(kernel, frames, heads_axis, groups), out...  365 us

profile of v2, /device:TPU:16, one launch (start us, length us, event | category | flops | bytes accessed | tf_op | source)
XLA Modules:
  0.0 372.3 jit_solution(14682911488823431872)
XLA Ops:
  0.0 1.4 reshape.38
  1.4 0.1 dynamic-slice_reduce_fusion
  1.6 0.2 fusion.1
  1.8 0.1 multiply_reduce_fusion
  1.9 0.5 broadcast_minimum_fusion.pick_ref
  2.4 0.1 copy.10
  2.5 0.6 dynamic-slice_reduce_fusion.3
  3.0 0.1 fusion
  3.1 0.8 broadcast_in_dim.15
  3.9 364.6 %shard_map.46 = bf16[4,128,3072]{2,1,0:T(8,128)(2,1)} custom-call(s32[16]{0:T(128)} %broadcast_minimum_fusion.pick_ref, f32[4,2,1,5120]{3,2,1,0:T(1,128)} %bitcast.7, bf16[4,128,3072]{2,1,0:T(8,128)(2,1)} %bitcast.9, bf16[4,128,3072]{2,1,0:T(8,128)(2,1)} %bitcast.10, bf16[4,128,3072]{2,1,0:T(8,128)(2,1)} %bitcast.11), custom_call_target="tpu_custom_call" | custom-call | flops 32212254720 | bytes 12582912 | tf_op jit(solution)/shard_map/pallas_call | solution.py:350
  368.6 3.8 %copy.13 = bf16[512,3072]{1,0:T(8,128)(2,1)} copy(bf16[512,3072]{1,0:T(8,128)(2,1)} %bitcast.6) | data formatting | bytes 6291456
  (2 shorter events, 0.0 us)
